TPU v7x, 128 devices: a whole 4x4x4 slice. The times are simulated.
128 devices in a mesh: lat: 4 (over z_hi, core), lon: 32 (over x, y, z_lo).
Axes of the slice: x: 4, y: 4, z: 4 (z_hi: 2, z_lo: 2; z = z_hi * 2 + z_lo), core: 2. Of those that a mesh axis runs over, the one named last changes fastest.
Arguments:
- terrain_surface: float32 [1024, 32768], P('lat', 'lon')
- azimuth_lag_tallies: int32 [8, 8], replicated, may hold values from 1 to 128, as said below
- holder_devices: int32 [524288, 1], P(('lat', 'lon')), may hold values from 0 to 127; in each aligned block of 4096 rows (0 to 4095, 4096 to 8191, ...) at most 128 rows name the same one
- holder_region_slot: int32 [524288], P(('lat', 'lon')), may hold values from 0 to 511
- footprint_weight: int32 [524288], P(('lat', 'lon')), may hold values from 1 to 64
Outputs:
- fine_svf: float32 [1024, 32768], P('lat', 'lon')
- cell_horizon: float32 [8, 65536], P(None, ('lat', 'lon'))
- cell_svf: float32 [65536], P(('lat', 'lon'))
Inputs may be any that keep to these rules, and one draw needn't show every extreme that they name: `holder_devices`: in the blocks of one device no owner is named by more than 128 blocks, a bound that some block reaches. `azimuth_lag_tallies`: every azimuth has a distance of 128.
All inputs are finite; a program needn't handle non-finite values.
Results may differ from a plain program's by a relative error of at most 0.0003.
Values sent between devices are 32-bit elements; how exact they have to be, the bound alone decides.
No kernel may reach another device: no remote copies, remote signals or barrier semaphores. Data moves between devices by JAX's collectives and lax.ppermute only.
A program may use at most 192 MiB of HBM per device.

v0:
```python
import jax
import jax.numpy as jnp
from jax import lax
from jax.sharding import PartitionSpec as P

FARTHEST_LAG = 128
AZ = 8
BY = 8
BX = 8
CELLS_DEV = 512


directions = ((0, 1), (1, 1), (1, 0), (1, -1), (0, -1), (-1, -1), (-1, 0), (-1, 1))
pixel_size = 92.6


def padded(shard, sides, width, wrap):
    for axis, dim in sides:
        devices, length = (lax.axis_size(axis), shard.shape[dim])
        up = [(i, (i + 1) % devices) for i in range(devices if wrap else devices - 1)]
        down = [(j, i) for i, j in up]
        last = lax.slice_in_dim(shard, length - width, length, axis=dim)
        first = lax.slice_in_dim(shard, 0, width, axis=dim)
        before = lax.ppermute(last, axis, up)
        after = lax.ppermute(first, axis, down)
        shard = jnp.concatenate([before, shard, after], axis=dim)
    return shard


def band_edges(haloed_altitude, northward_portion):
    position = lax.axis_index("lat")
    north_row = jnp.broadcast_to(
        haloed_altitude[FARTHEST_LAG : FARTHEST_LAG + 1], (FARTHEST_LAG, haloed_altitude.shape[1])
    )
    south_row = jnp.broadcast_to(
        haloed_altitude[FARTHEST_LAG + northward_portion - 1 : FARTHEST_LAG + northward_portion],
        (FARTHEST_LAG, haloed_altitude.shape[1]),
    )
    north = jnp.where(position == 0, north_row, haloed_altitude[:FARTHEST_LAG])
    south = jnp.where(
        position == lax.axis_size("lat") - 1,
        south_row,
        haloed_altitude[FARTHEST_LAG + northward_portion :],
    )
    return jnp.concatenate(
        [north, haloed_altitude[FARTHEST_LAG : FARTHEST_LAG + northward_portion], south], axis=0
    )


def block_means(field, northward_portion, eastward_portion):
    shaped = field.reshape(northward_portion // BY, BY, eastward_portion // BX, BX)
    return shaped.sum(axis=(1, 3)).reshape(-1) / (BY * BX)


def shards(
    terrain_surface, azimuth_lag_tallies, holder_devices, holder_region_slot, footprint_weight
):
    northward_portion, eastward_portion = terrain_surface.shape
    n_lat = lax.axis_size("lat")
    n_lon = lax.axis_size("lon")
    devices = n_lat * n_lon
    block_count = holder_devices.shape[0]
    capacity = max(2, 4 * block_count // devices)
    haloed_altitude = padded(terrain_surface, (("lat", 0),), FARTHEST_LAG, False)
    haloed_altitude = band_edges(haloed_altitude, northward_portion)
    haloed_altitude = padded(haloed_altitude, (("lon", 1),), FARTHEST_LAG, True)
    rows_global = (
        lax.axis_index("lat") * northward_portion + jnp.arange(northward_portion, dtype=jnp.int32)
    ).astype(jnp.float32)
    latitude = 47.0 - (rows_global + 0.5) / 1200.0
    coslat = jnp.cos(latitude * jnp.pi / 180.0)[:, None]
    weight = footprint_weight.astype(jnp.float32) / 64.0
    svf_total = jnp.zeros((northward_portion, eastward_portion), jnp.float32)
    angle_rows = []
    opening_rows = []
    for azimuth in range(AZ):
        step_y, step_x = directions[azimuth]
        observer_altitude = jnp.sqrt(
            (step_y * pixel_size) ** 2 + (step_x * pixel_size * coslat) ** 2
        )

        def sample(best, walking_offset):
            start_y = FARTHEST_LAG + step_y * walking_offset
            start_x = FARTHEST_LAG + step_x * walking_offset
            device_subgrid = lax.dynamic_slice(
                haloed_altitude, (start_y, start_x), (northward_portion, eastward_portion)
            )
            ascent_slope = (device_subgrid - terrain_surface) / (
                walking_offset.astype(jnp.float32) * observer_altitude
            )
            return (jnp.maximum(best, ascent_slope), None)

        best, unused = lax.scan(
            sample,
            jnp.full((northward_portion, eastward_portion), -jnp.inf, jnp.float32),
            azimuth_lag_tallies[azimuth],
        )
        rise = jnp.maximum(best, 0.0)
        angle = jnp.arctan(rise)
        opening = 1.0 / (1.0 + rise * rise)
        svf_total = svf_total + opening
        angle_rows.append(weight * block_means(angle, northward_portion, eastward_portion))
        opening_rows.append(weight * block_means(opening, northward_portion, eastward_portion))
    fine_svf = svf_total / AZ
    opening_count = len(opening_rows)
    features = jnp.stack(
        angle_rows + opening_rows + [weight, holder_region_slot.astype(jnp.float32)]
    )
    width = features.shape[0]
    owner = holder_devices[:, 0]
    member = (owner[:, None] == jnp.arange(devices, dtype=jnp.int32)[None, :]).astype(jnp.int32)
    earlier = jnp.cumsum(member, axis=0) - member
    slot_rank = jnp.sum(earlier * member, axis=1)
    target = owner * capacity + slot_rank
    outgoing = jnp.zeros((width, devices * capacity), jnp.float32).at[width - 1].set(-1.0)
    outgoing = outgoing.at[:, target].set(features)
    arrived = lax.all_to_all(
        outgoing.reshape(width, devices, capacity),
        ("lat", "lon"),
        split_axis=1,
        concat_axis=1,
        tiled=True,
    )
    grouped = arrived.reshape(width, devices // 8, 8 * capacity).transpose(1, 0, 2)
    cell_ids = jnp.arange(CELLS_DEV, dtype=jnp.float32)[None, :]

    def accumulate(totals, values):
        onehot = (values[width - 1][:, None] == cell_ids).astype(jnp.float32)
        added = jnp.dot(
            values[: width - 1],
            onehot,
            preferred_element_type=jnp.float32,
            precision=lax.Precision.HIGHEST,
        )
        return (totals + added, None)

    sums, unused = lax.scan(accumulate, jnp.zeros((width - 1, CELLS_DEV), jnp.float32), grouped)
    floor_area = jnp.maximum(sums[AZ + opening_count], 1.0)
    cell_horizon = sums[:AZ] / floor_area[None, :]
    cell_svf = jnp.sum(sums[AZ : AZ + opening_count], axis=0) / (AZ * floor_area)
    return (fine_svf, cell_horizon, cell_svf)


def solution(mesh):
    in_specs = (P("lat", "lon"), P(), P(("lat", "lon"), None), P(("lat", "lon")), P(("lat", "lon")))
    out_specs = (P("lat", "lon"), P(None, ("lat", "lon")), P(("lat", "lon")))
    return jax.shard_map(shards, mesh=mesh, in_specs=in_specs, out_specs=out_specs, check_vma=False)
```

profile of v0, /device:TPU:1, one launch (start us, length us, event | category | flops | bytes accessed | tf_op | source)
XLA Modules:
  0.0 766.9 jit_solution(6195903137437719913)
XLA Ops:
  6.3 5.5 collective-permute-start
  30.0 5.8 copy.83
  39.3 45.7 %while.116 = (s32[]{:T(128)}, f32[256,1024]{1,0:T(8,128)}, s32[8]{0:T(128)S(1)}, f32[512,1280]{1,0:T(8,128)}, f32[256,1024]{1,0:T(8,128)S(1)}, /*index=5*/s32[]{...) while((s32[]{:T(128)}, f32[256,1024]{1,0:T(8,128)}, s32[8]{0:T(128)S(1)}, ...), condition=%wide.region_1.2_spmd.clone, body=%wide.region_0.1_spmd.clone.sunk | while | flops 1050888 | bytes 4196541 | solution.py:93
  85.0 51.1 %while.117 = (s32[]{:T(128)}, f32[256,1024]{1,0:T(8,128)}, s32[8]{0:T(128)S(1)}, f32[512,1280]{1,0:T(8,128)}, f32[256,1024]{1,0:T(8,128)S(1)}, /*index=5*/s32[]{...) while((s32[]{:T(128)}, f32[256,1024]{1,0:T(8,128)}, ...), condition=%wide.region_3.4_spmd.clone, body=%wide.region_2.3_spmd.clone.sunk | while | flops 1051146 | bytes 4196578 | solution.py:93
  136.2 44.6 %while.118 = (s32[]{:T(128)}, f32[256,1024]{1,0:T(8,128)}, s32[8]{0:T(128)S(1)}, f32[512,1280]{1,0:T(8,128)}, f32[256,1024]{1,0:T(8,128)S(1)}, /*index=5*/s32[]{...) while((s32[]{:T(128)}, f32[256,1024]{1,0:T(8,128)}, s32[8]{0:T(128)S(1)}, ...), condition=%wide.region_5.6_spmd.clone, body=%wide.region_4.5_spmd.clone.sunk | while | flops 1051144 | bytes 4196541 | solution.py:93
  180.7 51.5 %while.119 = (s32[]{:T(128)}, f32[256,1024]{1,0:T(8,128)}, s32[8]{0:T(128)S(1)}, f32[512,1280]{1,0:T(8,128)}, f32[256,1024]{1,0:T(8,128)S(1)}, /*index=5*/s32[]{...) while((s32[]{:T(128)}, f32[256,1024]{1,0:T(8,128)}, ...), condition=%wide.region_7.8_spmd.clone, body=%wide.region_6.7_spmd.clone.sunk | while | flops 1051149 | bytes 4196619 | solution.py:93
  232.3 39.9 %while.120 = (s32[]{:T(128)}, f32[256,1024]{1,0:T(8,128)}, s32[8]{0:T(128)S(1)}, f32[512,1280]{1,0:T(8,128)}, f32[256,1024]{1,0:T(8,128)S(1)}, /*index=5*/s32[]{...) while((s32[]{:T(128)}, f32[256,1024]{1,0:T(8,128)}, ...), condition=%wide.region_9.10_spmd.clone, body=%wide.region_8.9_spmd.clone.sunk | while | flops 1050889 | bytes 4196561 | solution.py:93
  272.2 39.1 %while.121 = (s32[]{:T(128)}, f32[256,1024]{1,0:T(8,128)}, s32[8]{0:T(128)S(1)}, f32[512,1280]{1,0:T(8,128)}, f32[256,1024]{1,0:T(8,128)S(1)}, /*index=5*/s32[]{...) while((s32[]{:T(128)}, f32[256,1024]{1,0:T(8,128)}, ...), condition=%wide.region_11.12_spmd.clone, body=%wide.region_10.11_spmd.clone.sunk | while | flops 1051147 | bytes 4196598 | solution.py:93
  311.2 29.9 %while.122 = (s32[]{:T(128)}, f32[256,1024]{1,0:T(8,128)S(1)}, s32[8]{0:T(128)S(1)}, f32[512,1280]{1,0:T(8,128)}, f32[256,1024]{1,0:T(8,128)S(1)}, /*index=5*/s3...) while((s32[]{:T(128)}, f32[256,1024]{1,0:T(8,128)S(1)}, ...), condition=%wide.region_13.14_spmd.clone, body=%wide.region_12.13_spmd.clone.sunk | while | flops 1051145 | bytes 4196561 | solution.py:93
  341.2 43.7 %while.123 = (s32[]{:T(128)}, f32[256,1024]{1,0:T(8,128)S(1)}, s32[8]{0:T(128)S(1)}, f32[512,1280]{1,0:T(8,128)}, f32[256,1024]{1,0:T(8,128)S(1)}, /*index=5*/s3...) while((s32[]{:T(128)}, f32[256,1024]{1,0:T(8,128)S(1)}, ...), condition=%wide.region_15.16_spmd.clone, body=%wide.region_14.15_spmd.clone.sunk | while | flops 1051149 | bytes 4196619 | solution.py:93
  384.8 14.1 %add_divide_fusion = (f32[256,1024]{1,0:T(8,128)S(1)}, f32[256,1024]{1,0:T(8,128)}, f32[256,1024]{1,0:T(8,128)}, f32[256,1024]{1,0:T(8,128)}, f32[256,1024]{1,0:...) fusion(f32[256,1024]{1,0:T(8,128)S(1)} %get-tuple-element.664, ...), kind=kLoop, calls=%fused_computation.44 | loop fusion | flops 10485760 | bytes 26214400 | tf_op jit(solution)/shard_map/div | solution.py:100
  399.0 12.1 %reshape.375 = f32[32,8,128,8]{3,2,1,0:T(8,128)} reshape(f32[256,1024]{1,0:T(8,128)} %get-tuple-element.997) | data formatting | bytes 2097152 | tf_op jit(solution)/shard_map/reshape | solution.py:51
  411.1 11.3 %reshape.376 = f32[32,8,128,8]{3,2,1,0:T(8,128)} reshape(f32[256,1024]{1,0:T(8,128)S(1)} %copy-done.18) | data formatting | bytes 2097152 | tf_op jit(solution)/shard_map/reshape | solution.py:51
  422.4 6.9 reduce_sum.166
  429.3 7.0 reduce_sum.167
  436.4 11.2 %reshape.377 = f32[32,8,128,8]{3,2,1,0:T(8,128)} reshape(f32[256,1024]{1,0:T(8,128)S(1)} %copy-done.17) | data formatting | bytes 2097152 | tf_op jit(solution)/shard_map/reshape | solution.py:51
  447.6 7.0 reduce_sum.168
  454.6 11.2 %reshape.378 = f32[32,8,128,8]{3,2,1,0:T(8,128)} reshape(f32[256,1024]{1,0:T(8,128)S(1)} %copy-done.16) | data formatting | bytes 2097152 | tf_op jit(solution)/shard_map/reshape | solution.py:51
  465.8 7.0 reduce_sum.169
  472.8 11.2 %reshape.379 = f32[32,8,128,8]{3,2,1,0:T(8,128)} reshape(f32[256,1024]{1,0:T(8,128)S(1)} %copy-done.15) | data formatting | bytes 2097152 | tf_op jit(solution)/shard_map/reshape | solution.py:51
  484.0 7.0 reduce_sum.170
  491.0 11.2 %reshape.380 = f32[32,8,128,8]{3,2,1,0:T(8,128)} reshape(f32[256,1024]{1,0:T(8,128)S(1)} %copy-done.14) | data formatting | bytes 2097152 | tf_op jit(solution)/shard_map/reshape | solution.py:51
  502.2 7.0 reduce_sum.171
  509.2 11.3 %reshape.381 = f32[32,8,128,8]{3,2,1,0:T(8,128)} reshape(f32[256,1024]{1,0:T(8,128)S(1)} %copy-done.13) | data formatting | bytes 2097152 | tf_op jit(solution)/shard_map/reshape | solution.py:51
  520.6 7.0 reduce_sum.172
  527.6 11.2 %reshape.382 = f32[32,8,128,8]{3,2,1,0:T(8,128)} reshape(f32[256,1024]{1,0:T(8,128)S(1)} %copy-done.12) | data formatting | bytes 2097152 | tf_op jit(solution)/shard_map/reshape | solution.py:51
  538.8 7.0 reduce_sum.173
  545.8 11.2 %reshape.383 = f32[32,8,128,8]{3,2,1,0:T(8,128)} reshape(f32[256,1024]{1,0:T(8,128)S(1)} %copy-done.11) | data formatting | bytes 2097152 | tf_op jit(solution)/shard_map/reshape | solution.py:51
  557.0 7.0 reduce_sum.174
  564.0 11.2 %reshape.384 = f32[32,8,128,8]{3,2,1,0:T(8,128)} reshape(f32[256,1024]{1,0:T(8,128)S(1)} %copy-done.10) | data formatting | bytes 2097152 | tf_op jit(solution)/shard_map/reshape | solution.py:51
  575.2 7.0 reduce_sum.175
  582.2 11.2 %reshape.385 = f32[32,8,128,8]{3,2,1,0:T(8,128)} reshape(f32[256,1024]{1,0:T(8,128)S(1)} %copy-done.9) | data formatting | bytes 2097152 | tf_op jit(solution)/shard_map/reshape | solution.py:51
  593.4 7.0 reduce_sum.176
  600.4 11.2 %reshape.386 = f32[32,8,128,8]{3,2,1,0:T(8,128)} reshape(f32[256,1024]{1,0:T(8,128)S(1)} %copy-done.8) | data formatting | bytes 2097152 | tf_op jit(solution)/shard_map/reshape | solution.py:51
  611.6 7.0 reduce_sum.177
  618.7 11.4 %reshape.387 = f32[32,8,128,8]{3,2,1,0:T(8,128)} reshape(f32[256,1024]{1,0:T(8,128)S(1)} %copy-done.7) | data formatting | bytes 2097152 | tf_op jit(solution)/shard_map/reshape | solution.py:51
  630.1 7.0 reduce_sum.178
  637.1 11.2 %reshape.388 = f32[32,8,128,8]{3,2,1,0:T(8,128)} reshape(f32[256,1024]{1,0:T(8,128)S(1)} %copy-done.6) | data formatting | bytes 2097152 | tf_op jit(solution)/shard_map/reshape | solution.py:51
  648.3 7.0 reduce_sum.179
  655.3 11.2 %reshape.389 = f32[32,8,128,8]{3,2,1,0:T(8,128)} reshape(f32[256,1024]{1,0:T(8,128)S(1)} %copy-done.5) | data formatting | bytes 2097152 | tf_op jit(solution)/shard_map/reshape | solution.py:51
  666.5 6.9 reduce_sum.180
  673.4 11.2 %reshape.390 = f32[32,8,128,8]{3,2,1,0:T(8,128)} reshape(f32[256,1024]{1,0:T(8,128)S(1)} %get-tuple-element.982) | data formatting | bytes 2097152 | tf_op jit(solution)/shard_map/reshape | solution.py:51
  684.6 7.0 reduce_sum.181
  692.7 17.1 %scatter_fusion = f32[18,16384]{0,1:T(8,128)} fusion(f32[18,16384]{0,1:T(8,128)} %copy.83, s32[4096]{0:T(1024)S(1)} %bitcast.225, f32[4096,18]{1,0:T(8,128)S(1)} %copy.16), kind=kCustom, calls=%fused_computation | custom fusion | bytes 901120 | tf_op jit(solution)/shard_map/scatter | solution.py:116
  709.9 6.2 copy.17
  716.1 6.9 all-to-all-start
  723.1 25.0 %all-to-all-done = f32[18,128,128]{2,0,1:T(8,128)S(1)} async-done(((f32[18,128,128]{2,0,1:T(8,128)}), f32[18,128,128]{2,0,1:T(8,128)S(1)}, u32[]{:S(2)}, u32[]{:S(2)}) %all-to-all-start) | async-done | bytes 1179680 | tf_op jit(solution)/shard_map/all_to_all | solution.py:117
  750.7 14.5 %while.124 = (s32[]{:T(128)}, f32[17,512]{1,0:T(8,128)S(1)}, f32[16,18,1024]{2,0,1:T(8,128)S(1)}, s32[]{:T(128)}, s32[]{:T(128)}, /*index=5*/s32[]{}) while((s32[]{:T(128)}, f32[17,512]{1,0:T(8,128)S(1)}, f32[16,18,1024]{2,0,1:T(8,128)S(1)}, s32[]{:T(128)}, s32[]{:T(128)}, /*index=5*/s32[]{}) %tuple.318), condition=%wide.region_37.38_spmd.clone, body=%wide.region_36.37_spmd.clone.sunk | while | flops 107496448 | bytes 290919 | solution.py:137
  (331 shorter events, 264.5 us)
Async XLA Ops:
  2.9 16.2 %collective-permute-start.1 = (f32[128,1024]{1,0:T(8,128)}, f32[128,1024]{1,0:T(8,128)}, u32[]{:S(2)}, u32[]{:S(2)}) collective-permute-start(f32[128,1024]{1,0:T(8,128)} %get-tuple-element.1002), channel_id=1, source_target_pairs={{32,0},{64,32},{96,64},{33,1},{65,33},{97,65},{34,2},{66,34},{98,6... | collective-permute-start | bytes 1572872 | tf_op jit(solution)/shard_map/ppermute | solution.py:25
  6.3 14.0 %collective-permute-start = (f32[128,1024]{1,0:T(8,128)}, f32[128,1024]{1,0:T(8,128)}, u32[]{:S(2)}, u32[]{:S(2)}) collective-permute-start(f32[128,1024]{1,0:T(8,128)} %get-tuple-element.1001), channel_id=1, source_target_pairs={{0,32},{32,64},{64,96},{1,33},{33,65},{65,97},{2,34},{34,66},{66,9... | collective-permute-start | bytes 1572872 | tf_op jit(solution)/shard_map/ppermute | solution.py:24
  13.2 1.7 copy-start
  14.8 2.8 copy-start.19
  19.1 10.2 %copy-start.23 = (s32[4096]{0:T(1024)S(1)}, s32[4096]{0:T(1024)}, u32[]{:S(2)}) copy-start(s32[4096]{0:T(1024)} %param.28) | copy-start | bytes 49156
  20.3 1.3 copy-start.1
  21.6 1.0 copy-start.3
  22.6 13.2 %collective-permute-start.2 = (f32[512,128]{1,0:T(8,128)}, f32[512,128]{1,0:T(8,128)S(1)}, u32[]{:S(2)}, u32[]{:S(2)}) collective-permute-start(f32[512,128]{1,0:T(8,128)} %get-tuple-element.980), channel_id=1, source_target_pairs={{0,1},{1,2},{2,3},{3,4},{4,5},{5,6},{6,7},{7,8},{8,9},{9,10},{10,1... | collective-permute-start | bytes 786440 | tf_op jit(solution)/shard_map/ppermute | solution.py:24
  23.3 13.3 %collective-permute-start.3 = (f32[512,128]{1,0:T(8,128)}, f32[512,128]{1,0:T(8,128)}, u32[]{:S(2)}, u32[]{:S(2)}) collective-permute-start(f32[512,128]{1,0:T(8,128)} %get-tuple-element.981), channel_id=1, source_target_pairs={{1,0},{2,1},{3,2},{4,3},{5,4},{6,5},{7,6},{8,7},{9,8},{10,9},{11,1... | collective-permute-start | bytes 786440 | tf_op jit(solution)/shard_map/ppermute | solution.py:25
  29.9 5.8 copy-start.24
  29.9 6.7 copy-start.2
  30.0 6.7 copy-start.4
  398.9 12.1 %copy-start.18 = (f32[256,1024]{1,0:T(8,128)S(1)}, f32[256,1024]{1,0:T(8,128)}, u32[]{:S(2)}) copy-start(f32[256,1024]{1,0:T(8,128)} %get-tuple-element.996) | copy-start | bytes 3145732
  429.3 7.0 copy-start.17
  447.5 7.0 copy-start.16
  465.8 7.0 copy-start.15
  484.0 7.0 copy-start.14
  502.2 7.0 copy-start.13
  520.6 7.1 copy-start.12
  538.8 7.0 copy-start.11
  557.0 7.0 copy-start.10
  575.2 7.0 copy-start.9
  593.4 7.0 copy-start.8
  611.6 7.0 copy-start.7
  630.0 7.1 copy-start.6
  648.3 7.0 copy-start.5
  684.6 7.0 copy-start.22
  684.6 7.1 copy-start.21
  691.6 1.2 copy-start.20
  716.1 31.9 %all-to-all-start = ((f32[18,128,128]{2,0,1:T(8,128)}), f32[18,128,128]{2,0,1:T(8,128)S(1)}, u32[]{:S(2)}, u32[]{:S(2)}) async-start(f32[18,128,128]{2,0,1:T(8,128)} %copy.17), calls=%async_computation | async-start | bytes 3145728 | tf_op jit(solution)/shard_map/all_to_all | solution.py:117
where the time goes:
time: 775 us; the launch traced here: 767 us
  other arithmetic  316 us (41%)
  local copies, waits for them, and re-layouts  261 us (34%)
  loops' own time  128 us (17%)
  waiting for transfers between devices  25.9 us (3%)
  starting transfers between devices  21.9 us (3%)
  matrix products  12.7 us (2%)
    reshape x16, local copies, waits for them, and re-layouts, block_means(): field.reshape(northward_portion // BY, BY, eastward_portion // BX, BX)  180 us
    max x64, other arithmetic, sample(): return (jnp.maximum(best, ascent_slope), None)  173 us
    another operation x8, loops' own time, shards(): lax.scan(sample, jnp.full((northward_portion, eastward_portion), -jnp.inf...  127 us
    reduce_sum x16, other arithmetic, block_means(): return shaped.sum(axis=(1, 3)).reshape(-1) / (BY * BX)  112 us
    dynamic_slice x64, local copies, waits for them, and re-layouts, shards(): lax.scan(sample, jnp.full((northward_portion, eastward_portion), -jnp.inf...  40.9 us
    all_to_all x1, waiting for transfers between devices, shards(): lax.all_to_all(outgoing.reshape(width, devices, capacity), ('lat', 'lon')...  25 us
    scatter x1, local copies, waits for them, and re-layouts, shards(): outgoing = outgoing.at[:, target].set(features)  17.1 us
  transfers between devices with their start and end apart: 5, of which 2 were waited for; matrix products, arithmetic and copies ran while one was open for 2% of the time, Pallas kernels for 0%

commit v1 on v0

v1 whole, which is shorter than its diff:
```python
import jax
import jax.numpy as jnp
from jax import lax
from jax.experimental import pallas as pl
from jax.experimental.pallas import tpu as pltpu

FARTHEST_LAG = 128
AZ = 8
KS = 8
directions = ((0, 1), (1, 1), (1, 0), (1, -1), (0, -1), (-1, -1), (-1, 0), (-1, 1))
pixel_size = 92.6
ATAN = (0.9999999, -0.33331991, 0.19969724, -0.14019481, 0.09914293, -0.05948639, 0.0242524, -0.00469327)
HALF_PI = 1.5707963267948966


def recip(v):
    g = pl.reciprocal(v, approx=True)
    return g * (2.0 - v * g)


def quad_angle(r):
    x0, y0 = 1.0 - r[0] * r[1], r[0] + r[1]
    x1, y1 = 1.0 - r[2] * r[3], r[2] + r[3]
    x = x0 * x1 - y0 * y1
    y = x0 * y1 + x1 * y0
    ax, ay = jnp.abs(x), jnp.abs(y)
    z = jnp.minimum(ax, ay) * recip(jnp.maximum(ax, ay))
    u = z * z
    p = ATAN[7]
    for c in ATAN[6::-1]:
        p = p * u + c
    p = p * z
    p = jnp.where(ay > ax, HALF_PI - p, p)
    p = jnp.where(x < 0.0, 2.0 * HALF_PI - p, p)
    return jnp.where(y < 0.0, 4.0 * HALF_PI - p, p)


def sample_body(lags, inv_lags, invb, H, svf_ref, S, V, JW=4, PW=4):
    lane = lax.broadcasted_iota(jnp.int32, (8, 128), 1)
    nj = 8 // JW
    nph = 8 // PW

    def step(it, carry):
        rc = it // nj
        j0 = it % nj
        r0 = rc * 64
        jb = j0 * JW
        for ph in range(nph):
            ps = [ph * PW + p for p in range(PW)]
            t = [[H[jb + 1 + j, pl.ds(128 + r0 + p, 8, stride=8), :] for j in range(JW)] for p in ps]
            acc = [[None] * JW for _ in ps]
            for a in range(AZ):
                sy, sx = directions[a]
                best = [[None] * JW for _ in ps]
                for k in range(KS):
                    s = lags[a, k]
                    il = inv_lags[a, k]
                    row = 128 + r0 + sy * s
                    if sx == 1:
                        amount = 128 - s
                        keep = lane < amount
                    elif sx == -1:
                        amount = lax.bitwise_and(s, 127)
                        keep = lane < s
                    for pi, p in enumerate(ps):
                        if sx == 0:
                            got = [H[jb + 1 + j, pl.ds(row + p, 8, stride=8), :] for j in range(JW)]
                        else:
                            off = 1 if sx == 1 else 0
                            rolled = [
                                pltpu.roll(H[jb + j + off, pl.ds(row + p, 8, stride=8), :], amount, 1)
                                for j in range(JW + 1)
                            ]
                            got = [jnp.where(keep, rolled[j], rolled[j + 1]) for j in range(JW)]
                        for j in range(JW):
                            v = (got[j] - t[pi][j]) * il
                            best[pi][j] = v if k == 0 else jnp.maximum(best[pi][j], v)
                for pi, p in enumerate(ps):
                    if sx == 0:
                        ib = 1.0 / pixel_size
                    else:
                        ib = invb[0 if sy != 0 else 1, pl.ds(r0 + p, 8, stride=8), :]
                    for j in range(JW):
                        rise = jnp.minimum(jnp.maximum(best[pi][j] * ib, 0.0), 1e8)
                        best[pi][j] = rise
                        op = recip(1.0 + rise * rise)
                        acc[pi][j] = op if a == 0 else acc[pi][j] + op
                for j in range(JW):
                    th = None
                    for q in range(0, PW, 4):
                        th_q = quad_angle([best[q + i][j] for i in range(4)])
                        th = th_q if th is None else th + th_q
                    if ph == 0:
                        S[rc, a, jb + j] = th
                    else:
                        S[rc, a, jb + j] += th
            for j in range(JW):
                tot = None
                for pi, p in enumerate(ps):
                    sv = acc[pi][j] * (1.0 / AZ)
                    V[jb + j, pl.ds(r0 + p, 8, stride=8), :] = sv
                    tot = sv if tot is None else tot + sv
                if ph == 0:
                    S[rc, 8, jb + j] = tot
                else:
                    S[rc, 8, jb + j] += tot
        return carry

    lax.fori_loop(0, 4 * nj, step, 0)

N_DEV = 128
NBR = 32
CELLS_DEV = 512
F32 = jnp.float32
BF16 = jnp.bfloat16
VMEM = pl.BlockSpec(memory_space=pltpu.VMEM)
SMEM = pl.BlockSpec(memory_space=pltpu.SMEM)
NT = (((1,), (1,)), ((), ()))


def split2(v):
    hi = v.astype(BF16)
    return hi, (v - hi.astype(F32)).astype(BF16)


def iota(shape, dim):
    return lax.broadcasted_iota(jnp.int32, shape, dim)


def route_kernel(owner_ref, slot_ref, weight_ref, start_ref, index_ref, meta_ref, rank_ref):
    sub = iota((N_DEV, 128), 0)
    lane_row = iota((1, 128), 1)
    upper = (iota((128, 128), 0) < iota((128, 128), 1)).astype(BF16)
    right = jnp.concatenate([upper, jnp.ones((128, 128), BF16)], axis=1)
    count = jnp.zeros((N_DEV, 128), F32)
    for i in range(NBR):
        mine = sub == owner_ref[i : i + 1, :]
        both = jnp.dot(mine.astype(BF16), right, preferred_element_type=F32)
        rank = jnp.sum(jnp.where(mine, both[:, :128] + count, 0.0), axis=0, keepdims=True)
        rank_ref[i : i + 1, :] = rank
        count = count + both[:, 128:]
    lower = (iota((128, 128), 0) > iota((128, 128), 1)).astype(BF16)
    start = jnp.dot(lower, count.astype(BF16), preferred_element_type=F32)
    start_row = lax.dot_general(count[:, :8].T.astype(BF16), upper, (((1,), (0,)), ((), ())), preferred_element_type=F32)
    start_ref[...] = start_row[:1].astype(jnp.int32)
    inv = jnp.zeros((64, 128), F32)
    meta = jnp.zeros((3 * N_DEV, 128), F32)
    sub32 = iota((NBR, 128), 0)
    for i in range(NBR):
        mine = sub == owner_ref[i : i + 1, :]
        rank = rank_ref[i : i + 1, :]
        place = (rank + jnp.sum(jnp.where(mine, start, 0.0), axis=0, keepdims=True)).astype(jnp.int32)
        mine_hi = sub32 == lax.shift_right_logical(place, 7)
        lo_hot = (sub == lax.bitwise_and(place, 127)).astype(BF16)
        left = jnp.concatenate(
            [jnp.where(mine_hi, float(i), 0.0), jnp.where(mine_hi, lane_row.astype(F32), 0.0)], axis=0
        ).astype(BF16)
        inv = inv + lax.dot_general(left, lo_hot, NT, preferred_element_type=F32)
        rank_hot = (sub == rank.astype(jnp.int32)).astype(BF16)
        slot = slot_ref[i : i + 1, :] + 1
        parts = (lax.shift_right_logical(slot, 4), lax.bitwise_and(slot, 15), weight_ref[i : i + 1, :])
        left = jnp.concatenate([jnp.where(mine, v.astype(F32), 0.0) for v in parts], axis=0).astype(BF16)
        meta = meta + lax.dot_general(left, rank_hot, NT, preferred_element_type=F32)
    index_ref[...] = inv.astype(jnp.int32)
    meta_ref[0] = meta[:N_DEV] * 16.0 + meta[N_DEV : 2 * N_DEV]
    meta_ref[1] = meta[2 * N_DEV :]


def route(owner, slot, weight):
    return pl.pallas_call(
        route_kernel,
        name="route",
        out_shape=(
            jax.ShapeDtypeStruct((1, N_DEV), jnp.int32),
            jax.ShapeDtypeStruct((64, 128), jnp.int32),
            jax.ShapeDtypeStruct((2, N_DEV, 128), F32),
        ),
        in_specs=[VMEM] * 3,
        out_specs=[VMEM] * 3,
        scratch_shapes=[pltpu.VMEM((NBR, 128), F32)],
        cost_estimate=pl.CostEstimate(flops=int(4e8), bytes_accessed=200000, transcendentals=0),
    )(owner, slot, weight)


def main_kernel(
    lags, inv_lags, starts, lat, own, north, south, west, east, nw, ne, sw, se, invb, weight, index,
    svf_ref, feat_ref, open_ref, H, S, V, R, Z, Y,
):
    for j in range(8):
        c = slice(j * 128, (j + 1) * 128)
        H[1 + j, 0:128, :] = north[:, c]
        H[1 + j, 128:384, :] = own[:, c]
        H[1 + j, 384:512, :] = south[:, c]
    for c, parts in ((0, (nw, west, sw)), (9, (ne, east, se))):
        H[c, 0:128, :] = parts[0][...]
        H[c, 128:384, :] = parts[1][...]
        H[c, 384:512, :] = parts[2][...]

    @pl.when(lat[0] == 0)
    def _():
        for c in range(10):
            H[c, 0:128, :] = jnp.broadcast_to(H[c, 128:129, :], (128, 128))

    @pl.when(lat[0] == lat[1] - 1)
    def _():
        for c in range(10):
            H[c, 384:512, :] = jnp.broadcast_to(H[c, 383:384, :], (128, 128))

    sample_body(lags, inv_lags, invb, H, svf_ref, S, V)
    for j in range(8):
        svf_ref[:, j * 128 : (j + 1) * 128] = V[j]

    total = jnp.zeros((288, 128), F32)
    for j in range(8):
        pool = (iota((128, 128), 1) == j * 16 + lax.shift_right_logical(iota((128, 128), 0), 3)).astype(BF16)
        field = jnp.concatenate([S[rc, f, j] for rc in range(4) for f in range(9)], axis=0)
        hi, lo = split2(field)
        total = total + jnp.dot(hi, pool, preferred_element_type=F32) + jnp.dot(lo, pool, preferred_element_type=F32)
    R[...] = total
    sub = iota((8, 128), 0)
    lane = iota((8, 128), 1)
    scale = 1.0 / 4096.0
    for rc in range(4):
        for i in range(8):
            b = rc * 8 + i
            Y[b] = R[pl.ds(rc * 72 + i, 8, stride=8), :] * (weight[b : b + 1, :].astype(F32) * scale)
        Y[32 + rc] = R[rc * 72 + 64 : rc * 72 + 72, :] * (weight[rc * 8 : rc * 8 + 8, :].astype(F32) * scale)

    def gather(t, carry):
        hi = jnp.broadcast_to(index[pl.ds(t, 1), :], (8, 128))
        lo = jnp.broadcast_to(index[pl.ds(32 + t, 1), :], (8, 128))
        acc = jnp.zeros((8, 128), F32)
        for i in range(NBR):
            g = jnp.take_along_axis(Y[i], lo, axis=1, mode="promise_in_bounds")
            acc = jnp.where(hi == i, g, acc)
        Z[t, 0:8, :] = acc
        acc = jnp.zeros((8, 128), F32)
        for rc in range(4):
            g = jnp.take_along_axis(Y[32 + rc], lo, axis=1, mode="promise_in_bounds")
            acc = jnp.where(hi == rc * 8 + sub, g, acc)
        Z[t, 8:16, :] = jnp.broadcast_to(jnp.sum(acc, axis=0, keepdims=True), (8, 128))
        return carry

    lax.fori_loop(0, NBR, gather, 0)
    Z[32] = jnp.zeros((16, 128), F32)

    def expand(o, carry):
        st = starts[0, o]
        tile = lax.shift_right_logical(st, 7)
        q = 128 - lax.bitwise_and(st, 127)
        amount = lax.bitwise_and(q, 127)
        after = jnp.minimum(tile + 1, 32)
        tile = jnp.minimum(tile, 32)
        keep = lane < q
        for half in range(2):
            a = pltpu.roll(Z[tile, half * 8 : half * 8 + 8, :], amount, 1)
            b = pltpu.roll(Z[after, half * 8 : half * 8 + 8, :], amount, 1)
            got = jnp.where(keep, a, b)
            if half == 0:
                feat_ref[o] = got
            else:
                open_ref[pl.ds(o, 1), :] = got[0:1]
        return carry

    lax.fori_loop(0, N_DEV, expand, 0, unroll=4)


def main(*args):
    return pl.pallas_call(
        main_kernel,
        name="horizon",
        out_shape=(
            jax.ShapeDtypeStruct((256, 1024), F32),
            jax.ShapeDtypeStruct((N_DEV, 8, 128), F32),
            jax.ShapeDtypeStruct((N_DEV, 128), F32),
        ),
        in_specs=[SMEM] * 4 + [VMEM] * 12,
        out_specs=[VMEM] * 3,
        scratch_shapes=[
            pltpu.VMEM((10, 512, 128), F32),
            pltpu.VMEM((4, 9, 8, 8, 128), F32),
            pltpu.VMEM((8, 256, 128), F32),
            pltpu.VMEM((288, 128), F32),
            pltpu.VMEM((33, 16, 128), F32),
            pltpu.VMEM((36, 8, 128), F32),
        ],
        compiler_params=pltpu.CompilerParams(vmem_limit_bytes=40 * 1024 * 1024),
        cost_estimate=pl.CostEstimate(flops=int(1e10), bytes_accessed=6000000, transcendentals=0),
    )(*args)


def places_kernel(meta_ref, places_ref):
    valid = (meta_ref[0] > 0.0).astype(BF16)
    count = lax.dot_general(jnp.ones((8, 128), BF16), valid, NT, preferred_element_type=F32)
    upper = (iota((128, 128), 0) < iota((128, 128), 1)).astype(BF16)
    start = jnp.dot(count.astype(BF16), upper, preferred_element_type=F32)
    places_ref[0:1, :] = count[0:1].astype(jnp.int32)
    places_ref[1:2, :] = start[0:1].astype(jnp.int32)


def places(meta):
    return pl.pallas_call(
        places_kernel,
        name="places",
        out_shape=jax.ShapeDtypeStruct((2, N_DEV), jnp.int32),
        in_specs=[VMEM],
        out_specs=VMEM,
    )(meta)


def reduce_kernel(places_ref, meta_ref, feat_ref, open_ref, horizon_ref, svf_ref, C, M):
    lane = iota((8, 128), 1)
    M[pl.ds(0, N_DEV, stride=8), :] = open_ref[...]
    M[pl.ds(1, N_DEV, stride=8), :] = meta_ref[0]
    M[pl.ds(2, N_DEV, stride=8), :] = meta_ref[1]
    for r in range(3, 8):
        M[pl.ds(r, N_DEV, stride=8), :] = jnp.zeros((N_DEV, 128), F32)
    total = places_ref[1, N_DEV - 1] + places_ref[0, N_DEV - 1]
    chunks = lax.shift_right_logical(total + 255, 8)

    def clear(t, carry):
        C[2 * t] = jnp.zeros((16, 128), F32)
        C[2 * t + 1] = jnp.zeros((16, 128), F32)
        return carry

    lax.fori_loop(0, chunks + 1, clear, 0)

    def compact(src, carry):
        n = places_ref[0, src]
        st = places_ref[1, src]
        tile = lax.shift_right_logical(st, 7)
        q = lax.bitwise_and(st, 127)
        filled = lane < n
        first = lane >= q
        for half in range(2):
            v = feat_ref[src] if half == 0 else M[pl.ds(pl.multiple_of(src * 8, 8), 8), :]
            v = pltpu.roll(jnp.where(filled, v, 0.0), q, 1)
            rows = slice(half * 8, half * 8 + 8)
            C[tile, rows, :] += jnp.where(first, v, 0.0)
            C[tile + 1, rows, :] += jnp.where(first, 0.0, v)
        return carry

    lax.fori_loop(0, N_DEV, compact, 0)
    cell = (iota((CELLS_DEV, 256), 0) + 1).astype(F32)

    def accumulate(t, acc):
        pair = jnp.concatenate([C[2 * t], C[2 * t + 1]], axis=1)
        hi, lo = split2(pair)
        hot = (cell == pair[9:10, :]).astype(BF16)
        left = jnp.concatenate([hi, lo], axis=0)
        return acc + lax.dot_general(left, hot, NT, preferred_element_type=F32)

    acc = lax.fori_loop(0, chunks, accumulate, jnp.zeros((32, CELLS_DEV), F32))
    sums = acc[0:16] + acc[16:32]
    area = jnp.maximum(sums[10:11, :] * (1.0 / 64.0), 1.0)
    horizon_ref[...] = sums[0:8] / area
    svf_ref[...] = sums[8:9] / area


def reduce(*args):
    return pl.pallas_call(
        reduce_kernel,
        name="cells",
        out_shape=(jax.ShapeDtypeStruct((AZ, CELLS_DEV), F32), jax.ShapeDtypeStruct((1, CELLS_DEV), F32)),
        in_specs=[SMEM] + [VMEM] * 3,
        out_specs=[VMEM] * 2,
        scratch_shapes=[pltpu.VMEM((132, 16, 128), F32), pltpu.VMEM((8 * N_DEV, 128), F32)],
        compiler_params=pltpu.CompilerParams(vmem_limit_bytes=40 * 1024 * 1024),
    )(*args)


def shards(terrain_surface, azimuth_lag_tallies, holder_devices, holder_region_slot, footprint_weight):
    rows, cols = terrain_surface.shape
    n_lat = lax.axis_size("lat")
    n_lon = lax.axis_size("lon")
    W = FARTHEST_LAG

    def from_neighbour(block, dy, dx):
        pairs = []
        for la in range(n_lat):
            for lo in range(n_lon):
                if 0 <= la + dy < n_lat:
                    pairs.append(((la + dy) * n_lon + (lo + dx) % n_lon, la * n_lon + lo))
        return lax.ppermute(block, ("lat", "lon"), pairs)

    top, bottom = terrain_surface[:W], terrain_surface[rows - W :]
    north = from_neighbour(bottom, -1, 0)
    south = from_neighbour(top, 1, 0)
    west = from_neighbour(terrain_surface[:, cols - W :], 0, -1)
    east = from_neighbour(terrain_surface[:, :W], 0, 1)
    nw = from_neighbour(bottom[:, cols - W :], -1, -1)
    ne = from_neighbour(bottom[:, :W], -1, 1)
    sw = from_neighbour(top[:, cols - W :], 1, -1)
    se = from_neighbour(top[:, :W], 1, 1)

    start, index, meta = route(
        holder_devices.reshape(NBR, 128), holder_region_slot.reshape(NBR, 128), footprint_weight.reshape(NBR, 128)
    )
    meta = lax.all_to_all(meta, ("lat", "lon"), split_axis=1, concat_axis=1, tiled=True)

    rows_global = (lax.axis_index("lat") * rows + jnp.arange(rows, dtype=jnp.int32)).astype(F32)
    latitude = 47.0 - (rows_global + 0.5) / 1200.0
    coslat = jnp.cos(latitude * jnp.pi / 180.0)
    across = (pixel_size * coslat) ** 2
    inv_base = 1.0 / jnp.sqrt(jnp.stack([pixel_size**2 + across, across]))
    inv_base = jnp.broadcast_to(inv_base[:, :, None], (2, rows, 128))
    lat = jnp.stack([lax.axis_index("lat").astype(jnp.int32), jnp.int32(n_lat)])
    fine_svf, feats, opens = main(
        azimuth_lag_tallies, 1.0 / azimuth_lag_tallies.astype(F32), start, lat, terrain_surface,
        north, south, west, east, nw, ne, sw, se, inv_base, footprint_weight.reshape(NBR, 128), index,
    )
    where = places(meta)
    feats = lax.all_to_all(feats, ("lat", "lon"), split_axis=0, concat_axis=0, tiled=True)
    opens = lax.all_to_all(opens, ("lat", "lon"), split_axis=0, concat_axis=0, tiled=True)
    cell_horizon, cell_svf = reduce(where, meta, feats, opens)
    return fine_svf, cell_horizon, cell_svf.reshape(CELLS_DEV)


def solution(mesh):
    P = jax.sharding.PartitionSpec
    in_specs = (P("lat", "lon"), P(), P(("lat", "lon"), None), P(("lat", "lon")), P(("lat", "lon")))
    out_specs = (P("lat", "lon"), P(None, ("lat", "lon")), P(("lat", "lon")))
    return jax.shard_map(shards, mesh=mesh, in_specs=in_specs, out_specs=out_specs, check_vma=False)
```

time: 775 us -> 144 us (0.19)
  the two profiles are of different devices: /device:TPU:1 before, /device:TPU:49 now
where the time goes in v1:
time: 144 us; the launch traced here: 143 us
  Pallas kernels  61.3 us (43%)
  starting transfers between devices  42.4 us (29%)
  blocking collectives  18.1 us (13%)
  waiting for transfers between devices  12.6 us (9%)
  local copies, waits for them, and re-layouts  7.37 us (5%)
    pallas_call x1, Pallas kernels, main(): pl.pallas_call(main_kernel, name='horizon', out_shape=(jax.ShapeDtypeStru...  32.9 us
    pallas_call x1, Pallas kernels, reduce(): pl.pallas_call(reduce_kernel, name='cells', out_shape=(jax.ShapeDtypeStru...  22.6 us
    ppermute x8, starting transfers between devices, from_neighbour(): return lax.ppermute(block, ('lat', 'lon'), pairs)  22.5 us
    all_to_all x1, blocking collectives, shards(): lax.all_to_all(opens, ('lat', 'lon'), split_axis=0, concat_axis=0, tiled=...  18.1 us
    all_to_all x1, starting transfers between devices, shards(): lax.all_to_all(meta, ('lat', 'lon'), split_axis=1, concat_axis=1, tiled=T...  12.7 us
    all_to_all x1, waiting for transfers between devices, shards(): lax.all_to_all(feats, ('lat', 'lon'), split_axis=0, concat_axis=0, tiled=...  8.14 us
    all_to_all x1, starting transfers between devices, shards(): lax.all_to_all(feats, ('lat', 'lon'), split_axis=0, concat_axis=0, tiled=...  7.18 us
    ppermute x8, waiting for transfers between devices, from_neighbour(): return lax.ppermute(block, ('lat', 'lon'), pairs)  4.49 us
  transfers between devices with their start and end apart: 10, of which 2 were waited for; matrix products, arithmetic and copies ran while one was open for 3% of the time, Pallas kernels for 27%

profile of v1, /device:TPU:49, one launch (start us, length us, event | category | flops | bytes accessed | tf_op | source)
XLA Modules:
  0.0 142.8 jit_solution(10857090836811073274)
XLA Ops:
  0.6 1.6 %fusion = (f32[128,128]{1,0:T(8,128)S(1)}, f32[128,128]{1,0:T(8,128)}, f32[128,128]{1,0:T(8,128)}, f32[128,128]{1,0:T(8,128)}) fusion(f32[256,1024]{1,0:T(8,128)} %own.1), kind=kLoop, calls=%fused_computation.5 | loop fusion | bytes 524288 | tf_op jit(solution)/shard_map/slice | solution.py:394
  2.2 4.8 %collective-permute-start.4 = (f32[128,128]{1,0:T(8,128)}, f32[128,128]{1,0:T(8,128)S(1)}, u32[]{:S(2)}, u32[]{:S(2)}) collective-permute-start(f32[128,128]{1,0:T(8,128)} %get-tuple-element.22), channel_id=1, source_target_pairs={{31,32},{0,33},{1,34},{2,35},{3,36},{4,37},{5,38},{6,39},{7,40},{8... | collective-permute-start | bytes 196616 | tf_op jit(solution)/shard_map/ppermute | solution.py:384
  7.1 2.3 %collective-permute-start.5 = (f32[128,128]{1,0:T(8,128)}, f32[128,128]{1,0:T(8,128)S(1)}, u32[]{:S(2)}, u32[]{:S(2)}) collective-permute-start(f32[128,128]{1,0:T(8,128)} %get-tuple-element.21), channel_id=1, source_target_pairs={{1,32},{2,33},{3,34},{4,35},{5,36},{6,37},{7,38},{8,39},{9,40},{10... | collective-permute-start | bytes 196616 | tf_op jit(solution)/shard_map/ppermute | solution.py:384
  9.3 4.2 %collective-permute-start.6 = (f32[128,128]{1,0:T(8,128)}, f32[128,128]{1,0:T(8,128)S(1)}, u32[]{:S(2)}, u32[]{:S(2)}) collective-permute-start(f32[128,128]{1,0:T(8,128)} %get-tuple-element.20), channel_id=1, source_target_pairs={{63,0},{32,1},{33,2},{34,3},{35,4},{36,5},{37,6},{38,7},{39,8},{40... | collective-permute-start | bytes 196616 | tf_op jit(solution)/shard_map/ppermute | solution.py:384
  13.5 1.3 fusion.2
  14.8 0.0 copy-start
  14.8 4.2 %collective-permute-start = (f32[128,1024]{1,0:T(8,128)S(1)}, f32[128,1024]{1,0:T(8,128)S(1)}, u32[]{:S(2)}, u32[]{:S(2)}) collective-permute-start(f32[128,1024]{1,0:T(8,128)S(1)} %get-tuple-element.26), channel_id=1, source_target_pairs={{0,32},{1,33},{2,34},{3,35},{4,36},{5,37},{6,38},{7,39},{8,40},{9,... | collective-permute-start | bytes 1572872 | tf_op jit(solution)/shard_map/ppermute | solution.py:384
  19.0 1.9 %collective-permute-start.1 = (f32[128,1024]{1,0:T(8,128)S(1)}, f32[128,1024]{1,0:T(8,128)S(1)}, u32[]{:S(2)}, u32[]{:S(2)}) collective-permute-start(f32[128,1024]{1,0:T(8,128)S(1)} %get-tuple-element.25), channel_id=1, source_target_pairs={{32,0},{33,1},{34,2},{35,3},{36,4},{37,5},{38,6},{39,7},{40,8},{41... | collective-permute-start | bytes 1572872 | tf_op jit(solution)/shard_map/ppermute | solution.py:384
  20.9 4.0 %route.1 = (s32[1,128]{1,0:T(1,128)}, s32[64,128]{1,0:T(8,128)}, f32[2,128,128]{2,1,0:T(8,128)}) custom-call(s32[32,128]{1,0:T(8,128)} %bitcast.13, s32[32,128]{1,0:T(8,128)} %bitcast.14, s32[32,128]{1,0:T(8,128)} %bitcast.11), custom_call_target="tpu_custom_call" | custom-call | flops 400000000 | bytes 200000 | tf_op jit(solution)/shard_map/route/pallas_call | solution.py:170
  24.9 1.7 %copy.8 = f32[2,128,128]{2,0,1:T(2,128)} copy(f32[2,128,128]{2,1,0:T(8,128)} %get-tuple-element.14) | data formatting | bytes 262144 | tf_op jit(solution)/shard_map/route/pallas_call | solution.py:170
  26.6 12.7 %all-to-all-start = ((f32[2,128,128]{2,0,1:T(2,128)}), f32[2,128,128]{2,0,1:T(2,128)S(1)}, u32[]{:S(2)}, u32[]{:S(2)}) async-start(f32[2,128,128]{2,0,1:T(2,128)} %copy.8), calls=%async_computation | async-start | bytes 262144 | tf_op jit(solution)/shard_map/all_to_all | solution.py:399
  39.3 0.0 copy-done
  39.3 0.7 fusion.1
  40.0 0.0 copy-start.3
  40.0 0.7 copy-done.3
  40.7 0.1 multiply_multiply_fusion
  40.8 0.0 collective-permute-done.4.nw
  40.8 0.8 collective-permute-start.2
  41.6 0.0 collective-permute-done.5.ne
  41.6 0.8 collective-permute-start.3
  42.4 0.0 collective-permute-done.6.sw
  42.4 3.6 %collective-permute-start.7 = (f32[128,128]{1,0:T(8,128)S(1)}, f32[128,128]{1,0:T(8,128)S(1)}, u32[]{:S(2)}, u32[]{:S(2)}) collective-permute-start(f32[128,128]{1,0:T(8,128)S(1)} %get-tuple-element.19), channel_id=1, source_target_pairs={{33,0},{34,1},{35,2},{36,3},{37,4},{38,5},{39,6},{40,7},{41,8},{42... | collective-permute-start | bytes 196616 | tf_op jit(solution)/shard_map/ppermute | solution.py:384
  46.0 0.1 pad_add_fusion.lat
  46.1 0.0 copy-start.4
  46.1 0.0 copy-start.5
  46.1 4.5 %collective-permute-done.7.se = f32[128,128]{1,0:T(8,128)S(1)} collective-permute-done((f32[128,128]{1,0:T(8,128)S(1)}, f32[128,128]{1,0:T(8,128)S(1)}, u32[]{:S(2)}, u32[]{:S(2)}) %collective-permute-start.7) | collective-permute-done | bytes 65568 | tf_op jit(solution)/shard_map/ppermute | solution.py:384
  50.6 0.0 collective-permute-done.2.west
  50.6 0.0 collective-permute-done.3.east
  50.6 0.0 collective-permute-done.north
  50.6 0.0 collective-permute-done.1.south
  50.6 0.1 broadcast_in_dim.2.invb
  50.7 0.0 copy-start.6
  50.7 0.0 copy-done.4
  50.8 0.0 copy-done.5
  50.8 0.6 copy-done.6
  51.4 32.9 %horizon.1 = (f32[256,1024]{1,0:T(8,128)}, f32[128,8,128]{2,1,0:T(8,128)}, f32[128,128]{1,0:T(8,128)S(1)}) custom-call(s32[8,8]{1,0:T(8,128)S(1)} %copy-done.3, f32[8,8]{1,0:T(8,128)S(1)} %convert_divide_fusion.inv_lags, s32[1,128]{1,0:T(1,128)S(1)} %copy-done.6, s32[2]{0:T(128)S(1)} %pad_add_fusion.lat, f32[256,1024]{1,0:T(8,128)S(1)} %copy-done, ...), custom_call_target="tpu_custom_call" | custom-call | flops 10000000000 | bytes 6000000 | tf_op jit(solution)/shard_map/horizon/pallas_call | solution.py:269
  84.3 0.0 all-to-all-done
  84.3 18.1 %all_to_all.21 = f32[128,1,128]{2,1,0:T(1,128)S(1)} all-to-all(f32[128,1,128]{2,1,0:T(1,128)S(1)} %bitcast.10), channel_id=1, replica_groups=mesh['lat'=4,'lon'=32] {'lat','lon'}, dimensions={0} | all-to-all | bytes 131072 | tf_op jit(solution)/shard_map/all_to_all | solution.py:414
  102.4 7.2 %all-to-all-start.1 = ((f32[128,8,128]{2,1,0:T(8,128)}), f32[128,8,128]{2,1,0:T(8,128)S(1)}, u32[]{:S(2)}, u32[]{:S(2)}) async-start(f32[128,8,128]{2,1,0:T(8,128)} %get-tuple-element.15), calls=%async_computation.1 | async-start | bytes 1048576 | tf_op jit(solution)/shard_map/all_to_all | solution.py:413
  109.6 0.7 copy.9.meta_ref
  110.2 0.0 copy-start.1
  110.2 1.8 %places.1.places_ref = s32[2,128]{1,0:T(2,128)} custom-call(f32[2,128,128]{2,1,0:T(8,128)} %copy.9.meta_ref), custom_call_target="tpu_custom_call" | custom-call | tf_op jit(solution)/shard_map/places/pallas_call | solution.py:302
  112.0 0.0 copy-start.2
  112.0 8.1 %all-to-all-done.1.feat_ref = f32[128,8,128]{2,1,0:T(8,128)S(1)} async-done(((f32[128,8,128]{2,1,0:T(8,128)}), f32[128,8,128]{2,1,0:T(8,128)S(1)}, u32[]{:S(2)}, u32[]{:S(2)}) %all-to-all-start.1) | async-done | bytes 524320 | tf_op jit(solution)/shard_map/all_to_all | solution.py:413
  120.2 0.0 copy-done.1
  120.2 0.0 copy-done.2
  120.2 22.6 %cells.1 = (f32[8,512]{1,0:T(8,128)}, f32[1,512]{1,0:T(1,128)}) custom-call(s32[2,128]{1,0:T(2,128)S(1)} %copy-done.2, f32[2,128,128]{2,1,0:T(8,128)S(1)} %copy-done.1, f32[128,8,128]{2,1,0:T(8,128)S(1)} %all-to-all-done.1.feat_ref, f32[128,128]{1,0:T(8,128)S(1)} %bitcast.9), custom_call_target="tpu_custom_call" | custom-call | tf_op jit(solution)/shard_map/cells/pallas_call | solution.py:361
  (2 shorter events, 0.0 us)
Async XLA Ops:
  2.2 38.6 %collective-permute-start.4 = (f32[128,128]{1,0:T(8,128)}, f32[128,128]{1,0:T(8,128)S(1)}, u32[]{:S(2)}, u32[]{:S(2)}) collective-permute-start(f32[128,128]{1,0:T(8,128)} %get-tuple-element.22), channel_id=1, source_target_pairs={{31,32},{0,33},{1,34},{2,35},{3,36},{4,37},{5,38},{6,39},{7,40},{8... | collective-permute-start | bytes 196616 | tf_op jit(solution)/shard_map/ppermute | solution.py:384
  7.1 34.5 %collective-permute-start.5 = (f32[128,128]{1,0:T(8,128)}, f32[128,128]{1,0:T(8,128)S(1)}, u32[]{:S(2)}, u32[]{:S(2)}) collective-permute-start(f32[128,128]{1,0:T(8,128)} %get-tuple-element.21), channel_id=1, source_target_pairs={{1,32},{2,33},{3,34},{4,35},{5,36},{6,37},{7,38},{8,39},{9,40},{10... | collective-permute-start | bytes 196616 | tf_op jit(solution)/shard_map/ppermute | solution.py:384
  9.3 33.0 %collective-permute-start.6 = (f32[128,128]{1,0:T(8,128)}, f32[128,128]{1,0:T(8,128)S(1)}, u32[]{:S(2)}, u32[]{:S(2)}) collective-permute-start(f32[128,128]{1,0:T(8,128)} %get-tuple-element.20), channel_id=1, source_target_pairs={{63,0},{32,1},{33,2},{34,3},{35,4},{36,5},{37,6},{38,7},{39,8},{40... | collective-permute-start | bytes 196616 | tf_op jit(solution)/shard_map/ppermute | solution.py:384
  14.8 24.5 %copy-start = (f32[256,1024]{1,0:T(8,128)S(1)}, f32[256,1024]{1,0:T(8,128)}, u32[]{:S(2)}) copy-start(f32[256,1024]{1,0:T(8,128)} %own.1) | copy-start | bytes 3145732
  14.8 35.8 %collective-permute-start = (f32[128,1024]{1,0:T(8,128)S(1)}, f32[128,1024]{1,0:T(8,128)S(1)}, u32[]{:S(2)}, u32[]{:S(2)}) collective-permute-start(f32[128,1024]{1,0:T(8,128)S(1)} %get-tuple-element.26), channel_id=1, source_target_pairs={{0,32},{1,33},{2,34},{3,35},{4,36},{5,37},{6,38},{7,39},{8,40},{9,... | collective-permute-start | bytes 1572872 | tf_op jit(solution)/shard_map/ppermute | solution.py:384
  19.0 31.6 %collective-permute-start.1 = (f32[128,1024]{1,0:T(8,128)S(1)}, f32[128,1024]{1,0:T(8,128)S(1)}, u32[]{:S(2)}, u32[]{:S(2)}) collective-permute-start(f32[128,1024]{1,0:T(8,128)S(1)} %get-tuple-element.25), channel_id=1, source_target_pairs={{32,0},{33,1},{34,2},{35,3},{36,4},{37,5},{38,6},{39,7},{40,8},{41... | collective-permute-start | bytes 1572872 | tf_op jit(solution)/shard_map/ppermute | solution.py:384
  26.6 57.7 %all-to-all-start = ((f32[2,128,128]{2,0,1:T(2,128)}), f32[2,128,128]{2,0,1:T(2,128)S(1)}, u32[]{:S(2)}, u32[]{:S(2)}) async-start(f32[2,128,128]{2,0,1:T(2,128)} %copy.8), calls=%async_computation | async-start | bytes 262144 | tf_op jit(solution)/shard_map/all_to_all | solution.py:399
  40.0 0.7 copy-start.3
  40.8 9.8 %collective-permute-start.2 = (f32[256,128]{1,0:T(8,128)}, f32[256,128]{1,0:T(8,128)S(1)}, u32[]{:S(2)}, u32[]{:S(2)}) collective-permute-start(f32[256,128]{1,0:T(8,128)} %get-tuple-element.24), channel_id=1, source_target_pairs={{31,0},{0,1},{1,2},{2,3},{3,4},{4,5},{5,6},{6,7},{7,8},{8,9},{9,10... | collective-permute-start | bytes 393224 | tf_op jit(solution)/shard_map/ppermute | solution.py:384
  41.6 9.0 %collective-permute-start.3 = (f32[256,128]{1,0:T(8,128)}, f32[256,128]{1,0:T(8,128)S(1)}, u32[]{:S(2)}, u32[]{:S(2)}) collective-permute-start(f32[256,128]{1,0:T(8,128)} %get-tuple-element.23), channel_id=1, source_target_pairs={{1,0},{2,1},{3,2},{4,3},{5,4},{6,5},{7,6},{8,7},{9,8},{10,9},{11,1... | collective-permute-start | bytes 393224 | tf_op jit(solution)/shard_map/ppermute | solution.py:384
  42.4 8.2 %collective-permute-start.7 = (f32[128,128]{1,0:T(8,128)S(1)}, f32[128,128]{1,0:T(8,128)S(1)}, u32[]{:S(2)}, u32[]{:S(2)}) collective-permute-start(f32[128,128]{1,0:T(8,128)S(1)} %get-tuple-element.19), channel_id=1, source_target_pairs={{33,0},{34,1},{35,2},{36,3},{37,4},{38,5},{39,6},{40,7},{41,8},{42... | collective-permute-start | bytes 196616 | tf_op jit(solution)/shard_map/ppermute | solution.py:384
  46.1 4.6 %copy-start.4 = (s32[4096]{0:T(1024)S(1)}, s32[4096]{0:T(1024)}, u32[]{:S(2)}) copy-start(s32[4096]{0:T(1024)} %param.9) | copy-start | bytes 49156
  46.1 4.7 %copy-start.5 = (s32[64,128]{1,0:T(8,128)S(1)}, s32[64,128]{1,0:T(8,128)}, u32[]{:S(2)}) copy-start(s32[64,128]{1,0:T(8,128)} %get-tuple-element.12.index) | copy-start | bytes 98308
  50.7 0.7 copy-start.6
  102.4 17.8 %all-to-all-start.1 = ((f32[128,8,128]{2,1,0:T(8,128)}), f32[128,8,128]{2,1,0:T(8,128)S(1)}, u32[]{:S(2)}, u32[]{:S(2)}) async-start(f32[128,8,128]{2,1,0:T(8,128)} %get-tuple-element.15), calls=%async_computation.1 | async-start | bytes 1048576 | tf_op jit(solution)/shard_map/all_to_all | solution.py:413
  110.2 9.9 %copy-start.1 = (f32[2,128,128]{2,1,0:T(8,128)S(1)}, f32[2,128,128]{2,1,0:T(8,128)}, u32[]{:S(2)}) copy-start(f32[2,128,128]{2,1,0:T(8,128)} %copy.9.meta_ref) | copy-start | bytes 393220
  112.0 8.1 %copy-start.2 = (s32[2,128]{1,0:T(2,128)S(1)}, s32[2,128]{1,0:T(2,128)}, u32[]{:S(2)}) copy-start(s32[2,128]{1,0:T(2,128)} %places.1.places_ref) | copy-start | bytes 3076
